TPU v7x, 32 devices: a whole 2x2x4 slice. The times are simulated.
32 devices in a mesh: dp: 8 (over y, x, core), tensor: 4 (over z).
Axes of the slice: x: 2, y: 2, z: 4, core: 2. Of those that a mesh axis runs over, the one named last changes fastest.
Arguments:
- tokens: bfloat16 [1024, 8, 1024], P('tensor', 'dp'), may hold values from -6 to 6
- cotangent: bfloat16 [1024, 8, 1024], P('tensor', 'dp'), may hold values from -6 to 6
- clip_mask: int32 [8], P('dp'), may hold values from 0 to 1, as said below
- positions: int32 [3, 8, 1024], P(None, 'dp'), may hold values from 0 to 15
- triple_weight: bfloat16 [2, 1024, 3, 1024], P(None, 'dp', None, 'tensor'), may hold values from -0.1875 to 0.1875
- triple_bias: bfloat16 [2, 3, 1024], P(None, None, 'tensor'), may hold values from -0.75 to 0.75
- exit_weight: bfloat16 [2, 1024, 1024], P(None, 'tensor', 'dp'), may hold values from -2 to 2
- expand_weight: bfloat16 [2, 1024, 4096], P(None, 'dp', 'tensor'), may hold values from -0.1875 to 0.1875
- expand_bias: bfloat16 [2, 4096], P(None, 'tensor'), may hold values from -4 to 4
- shrink_weight: bfloat16 [2, 4096, 1024], P(None, 'tensor', 'dp'), may hold values from -0.09375 to 0.09375
- norm_gain: bfloat16 [2, 2, 1024], replicated, may hold values from 0.5 to 1.5
- norm_shift: bfloat16 [2, 2, 1024], replicated, may hold values from -3 to 3
- branch_bias: bfloat16 [2, 2, 1024], replicated, may hold values from -4 to 4
Outputs:
- mixed: float32 [1024, 8, 1024], P('tensor', 'dp')
- tokens_gradient: float32 [1024, 8, 1024], P('tensor', 'dp')
- triple_gradient: float32 [2, 1024, 3, 1024], P(None, 'dp', None, 'tensor')
- triple_bias_gradient: float32 [2, 3, 1024], P(None, None, 'tensor')
- exit_gradient: float32 [2, 1024, 1024], P(None, 'tensor', 'dp')
- expand_gradient: float32 [2, 1024, 4096], P(None, 'dp', 'tensor')
- expand_bias_gradient: float32 [2, 4096], P(None, 'tensor')
- shrink_gradient: float32 [2, 4096, 1024], P(None, 'tensor', 'dp')
- gain_gradient: float32 [2, 2, 1024], replicated
- shift_gradient: float32 [2, 2, 1024], replicated
- branch_bias_gradient: float32 [2, 2, 1024], replicated
Inputs may be any that keep to these rules, and one draw needn't show every extreme that they name: `clip_mask`: exactly 1 of the 8 slots hold 0.
All inputs are finite; a program needn't handle non-finite values.
Results may differ from a plain program's by a relative error of at most 0.015.
Values may be sent and summed in bfloat16 or wider, within the bound.
A program may use at most 128 MiB of HBM per device.

v0:
```python
import jax
import jax.numpy as jnp
from jax import lax
from jax.sharding import PartitionSpec as P

HEAD_DIM = 64
ROT = 20
LAYERS = 2
SEQ = 1024
QBLOCK = 512
EPSILON = 1e-06
SQRT_HALF = 0.7071067811865476
ROOT_TWO_PI = 2.5066282746310002


def rotary_tables(positions):
    halfway = ROT // 2
    indices = jnp.arange(halfway, dtype=jnp.float32)
    frequency = 10000.0 ** (-indices / halfway)
    angles = jnp.transpose(positions.astype(jnp.float32), (0, 2, 1))[..., None] * frequency
    return (jnp.cos(angles)[:, :, :, None, :], jnp.sin(angles)[:, :, :, None, :])


def rotate(values, cosines, sines):
    halfway = ROT // 2
    pieces = []
    for coord_index in range(3):
        offset = coord_index * ROT
        former = values[..., offset : offset + halfway]
        latter = values[..., offset + halfway : offset + ROT]
        pieces.append(former * cosines[coord_index] - latter * sines[coord_index])
        pieces.append(latter * cosines[coord_index] + former * sines[coord_index])
    pieces.append(values[..., 3 * ROT :])
    return jnp.concatenate(pieces, axis=-1)


def normalize(values, gain_row, shift_row):
    center = values - jnp.mean(values, axis=-1, keepdims=True)
    inverse = lax.rsqrt(jnp.mean(center * center, axis=-1, keepdims=True) + EPSILON)
    scaled = center * inverse
    return (scaled * gain_row + shift_row, scaled, inverse)


def norm_back(upstream, scaled, inverse, gain_row):
    weighted = upstream * gain_row
    first_mean = jnp.mean(weighted, axis=-1, keepdims=True)
    second_mean = jnp.mean(weighted * scaled, axis=-1, keepdims=True)
    return inverse * (weighted - first_mean - scaled * second_mean)


def gelu_slope(inner_sum):
    return (
        0.5 * (1.0 + lax.erf(inner_sum * SQRT_HALF))
        + inner_sum * jnp.exp(-0.5 * inner_sum * inner_sum) / ROOT_TWO_PI
    )


def to_items(array):
    seq_length, clip_count, head_count, head_width = array.shape
    return jnp.transpose(array, (1, 2, 0, 3)).reshape(
        clip_count * head_count, seq_length, head_width
    )


def from_items(array, clip_count):
    item_count, seq_length, head_width = array.shape
    return jnp.transpose(
        array.reshape(clip_count, item_count // clip_count, seq_length, head_width), (2, 0, 1, 3)
    )


def attend(queries, key_items, values):
    factor = HEAD_DIM ** (-0.5)
    block_count = SEQ // QBLOCK

    def one_item(triple):
        query_rows, key_rows, value_rows = triple

        def one_block(query_block):
            scores = (
                jnp.einsum("qe,ke->qk", query_block, key_rows, preferred_element_type=jnp.float32)
                * factor
            )
            highest = jnp.max(scores, axis=-1, keepdims=True)
            weights = jnp.exp(scores - highest)
            summed = jnp.sum(weights, axis=-1, keepdims=True)
            chances = (weights / summed).astype(jnp.bfloat16)
            output = jnp.einsum(
                "qk,ke->qe", chances, value_rows, preferred_element_type=jnp.float32
            )
            return (output.astype(jnp.bfloat16), (highest + jnp.log(summed))[:, 0])

        outputs, logsums = lax.map(one_block, query_rows.reshape(block_count, QBLOCK, HEAD_DIM))
        return (outputs.reshape(SEQ, HEAD_DIM), logsums.reshape(SEQ))

    return lax.map(one_item, (queries, key_items, values))


def attend_back(queries, key_items, values, out_grads, logsums):
    factor = HEAD_DIM ** (-0.5)
    block_count = SEQ // QBLOCK

    def one_item(group):
        query_rows, key_rows, value_rows, grad_rows, logsum_rows = group

        def one_block(carry, blocked):
            key_total, value_total = carry
            query_block, grad_block, logsum_block = blocked
            scores = (
                jnp.einsum("qe,ke->qk", query_block, key_rows, preferred_element_type=jnp.float32)
                * factor
            )
            chances = jnp.exp(scores - logsum_block[:, None])
            value_total = value_total + jnp.einsum(
                "qk,qe->ke",
                chances.astype(jnp.bfloat16),
                grad_block,
                preferred_element_type=jnp.float32,
            )
            chance_grad = jnp.einsum(
                "qe,ke->qk", grad_block, value_rows, preferred_element_type=jnp.float32
            )
            center = jnp.sum(chances * chance_grad, axis=-1, keepdims=True)
            score_grad = (chances * (chance_grad - center)).astype(jnp.bfloat16)
            query_grad = (
                jnp.einsum("qk,ke->qe", score_grad, key_rows, preferred_element_type=jnp.float32)
                * factor
            )
            key_total = (
                key_total
                + jnp.einsum(
                    "qk,qe->ke", score_grad, query_block, preferred_element_type=jnp.float32
                )
                * factor
            )
            return ((key_total, value_total), query_grad)

        zeros = jnp.zeros((SEQ, HEAD_DIM), jnp.float32)
        blocked_rows = (
            query_rows.reshape(block_count, QBLOCK, HEAD_DIM),
            grad_rows.reshape(block_count, QBLOCK, HEAD_DIM),
            logsum_rows.reshape(block_count, QBLOCK),
        )
        (key_total, value_total), query_grads = lax.scan(one_block, (zeros, zeros), blocked_rows)
        return (query_grads.reshape(SEQ, HEAD_DIM), key_total, value_total)

    return lax.map(one_item, (queries, key_items, values, out_grads, logsums))


def shards(
    tokens,
    cotangent,
    clip_mask,
    positions,
    triple_weight,
    triple_bias,
    exit_weight,
    expand_weight,
    expand_bias,
    shrink_weight,
    norm_gain,
    norm_shift,
    branch_bias,
):
    row_count = tokens.shape[0]
    clip_count = tokens.shape[1]
    local_width = triple_weight.shape[3]
    head_count = local_width // HEAD_DIM
    cosines, sines = rotary_tables(positions)
    live = clip_mask.astype(jnp.float32)[None, :, None]

    def spread_rows(normed):
        return lax.all_gather(normed, "tensor", axis=0, tiled=True)

    def spread_grads(upstream_low):
        return lax.all_gather(upstream_low, "tensor", axis=0, tiled=True)

    def collect_rows(operand, matrix, pattern):

        def partial_term(offset, row_span):
            return jnp.einsum(pattern, operand, matrix, preferred_element_type=jnp.float32)

        return lax.psum_scatter(
            partial_term(jnp.int32(0), row_count * lax.axis_size("tensor")).astype(jnp.bfloat16),
            "tensor",
            scatter_dimension=0,
            tiled=True,
        ).astype(jnp.float32)

    def collect_grads(operand, matrix, pattern):

        def partial_term(offset, row_span):
            return jnp.einsum(pattern, operand, matrix, preferred_element_type=jnp.float32)

        return lax.psum_scatter(
            partial_term(jnp.int32(0), row_count * lax.axis_size("tensor")).astype(jnp.bfloat16),
            "tensor",
            scatter_dimension=0,
            tiled=True,
        ).astype(jnp.float32)

    hidden = tokens.astype(jnp.float32)
    saved = []
    for layer_index in range(LAYERS):
        fetched = (
            lax.all_gather(triple_weight[layer_index], "dp", axis=0, tiled=True),
            lax.all_gather(exit_weight[layer_index], "dp", axis=1, tiled=True),
            lax.all_gather(expand_weight[layer_index], "dp", axis=0, tiled=True),
            lax.all_gather(shrink_weight[layer_index], "dp", axis=1, tiled=True),
        )
        triple_full, exit_full, expand_full, shrink_full = fetched
        gain_pair = norm_gain[layer_index].astype(jnp.float32)
        shift_pair = norm_shift[layer_index].astype(jnp.float32)
        bias_pair = branch_bias[layer_index].astype(jnp.float32)
        normed, scaled_one, inverse_one = normalize(hidden, gain_pair[0], shift_pair[0])
        gathered_one = spread_rows(normed.astype(jnp.bfloat16))
        mixed_triple = jnp.einsum(
            "scd,dtf->sctf", gathered_one, triple_full, preferred_element_type=jnp.float32
        ) + triple_bias[layer_index].astype(jnp.float32)
        split_heads = mixed_triple.reshape(SEQ, clip_count, 3, head_count, HEAD_DIM)
        query_items = to_items(rotate(split_heads[:, :, 0], cosines, sines).astype(jnp.bfloat16))
        key_items = to_items(rotate(split_heads[:, :, 1], cosines, sines).astype(jnp.bfloat16))
        value_items = to_items(split_heads[:, :, 2].astype(jnp.bfloat16))
        attended_items, logsums = attend(query_items, key_items, value_items)
        attended = from_items(attended_items, clip_count).reshape(SEQ, clip_count, local_width)
        hidden = hidden + (collect_rows(attended, exit_full, "sce,ed->scd") + bias_pair[0])
        normed, scaled_two, inverse_two = normalize(hidden, gain_pair[1], shift_pair[1])
        gathered_two = spread_rows(normed.astype(jnp.bfloat16))
        inner_sum = jnp.einsum(
            "scd,df->scf", gathered_two, expand_full, preferred_element_type=jnp.float32
        ) + expand_bias[layer_index].astype(jnp.float32)
        activated = jax.nn.gelu(inner_sum, approximate=False).astype(jnp.bfloat16)
        hidden = hidden + (collect_rows(activated, shrink_full, "scf,fd->scd") + bias_pair[1])
        saved.append(
            (
                gathered_one,
                scaled_one,
                inverse_one,
                query_items,
                key_items,
                value_items,
                logsums,
                attended,
                scaled_two,
                inverse_two,
                gathered_two,
                inner_sum,
                activated,
                fetched,
            )
        )
    mixed = hidden * live
    upstream = cotangent.astype(jnp.float32) * live
    collected = [None] * LAYERS
    gain_parts = [None] * LAYERS
    shift_parts = [None] * LAYERS
    bias_parts = [None] * LAYERS
    triple_bias_parts = [None] * LAYERS
    expand_bias_parts = [None] * LAYERS
    for layer_index in reversed(range(LAYERS)):
        (
            gathered_one,
            scaled_one,
            inverse_one,
            query_items,
            key_items,
            value_items,
            logsums,
            attended,
            scaled_two,
            inverse_two,
            gathered_two,
            inner_sum,
            activated,
            fetched,
        ) = saved[layer_index]
        triple_full, exit_full, expand_full, shrink_full = (
            lax.all_gather(triple_weight[layer_index], "dp", axis=0, tiled=True),
            lax.all_gather(exit_weight[layer_index], "dp", axis=1, tiled=True),
            lax.all_gather(expand_weight[layer_index], "dp", axis=0, tiled=True),
            lax.all_gather(shrink_weight[layer_index], "dp", axis=1, tiled=True),
        )
        gain_pair = norm_gain[layer_index].astype(jnp.float32)
        shrink_low = upstream.astype(jnp.bfloat16)
        bias_two = jnp.sum(shrink_low, axis=(0, 1), dtype=jnp.float32)
        full_grad = spread_grads(shrink_low)
        shrink_grad = jnp.einsum(
            "scf,scd->fd", activated, full_grad, preferred_element_type=jnp.float32
        )
        active_grad = jnp.einsum(
            "scd,fd->scf", full_grad, shrink_full, preferred_element_type=jnp.float32
        )
        inner_low = (active_grad * gelu_slope(inner_sum)).astype(jnp.bfloat16)
        expand_bias_parts[layer_index] = jnp.sum(inner_low, axis=(0, 1), dtype=jnp.float32)
        expand_grad = jnp.einsum(
            "scd,scf->df", gathered_two, inner_low, preferred_element_type=jnp.float32
        )
        normed_grad = collect_grads(inner_low, expand_full, "scf,df->scd")
        gain_two = jnp.sum(normed_grad * scaled_two, axis=(0, 1))
        shift_two = jnp.sum(normed_grad, axis=(0, 1))
        upstream = upstream + norm_back(normed_grad, scaled_two, inverse_two, gain_pair[1])
        branch_low = upstream.astype(jnp.bfloat16)
        bias_one = jnp.sum(branch_low, axis=(0, 1), dtype=jnp.float32)
        full_grad = spread_grads(branch_low)
        exit_grad = jnp.einsum(
            "sce,scd->ed", attended, full_grad, preferred_element_type=jnp.float32
        )
        attended_grad = jnp.einsum(
            "scd,ed->sce", full_grad, exit_full, preferred_element_type=jnp.float32
        ).astype(jnp.bfloat16)
        grad_items = to_items(attended_grad.reshape(SEQ, clip_count, head_count, HEAD_DIM))
        query_grad, key_grad, value_grad = attend_back(
            query_items, key_items, value_items, grad_items, logsums
        )
        query_back = rotate(from_items(query_grad, clip_count), cosines, -sines)
        key_back = rotate(from_items(key_grad, clip_count), cosines, -sines)
        value_back = from_items(value_grad, clip_count)
        triple_low = (
            jnp.stack([query_back, key_back, value_back], axis=2)
            .reshape(SEQ, clip_count, 3, local_width)
            .astype(jnp.bfloat16)
        )
        triple_bias_parts[layer_index] = jnp.sum(triple_low, axis=(0, 1), dtype=jnp.float32)
        triple_grad = jnp.einsum(
            "scd,sctf->dtf", gathered_one, triple_low, preferred_element_type=jnp.float32
        )
        normed_grad = collect_grads(triple_low, triple_full, "sctf,dtf->scd")
        gain_one = jnp.sum(normed_grad * scaled_one, axis=(0, 1))
        shift_one = jnp.sum(normed_grad, axis=(0, 1))
        upstream = upstream + norm_back(normed_grad, scaled_one, inverse_one, gain_pair[0])
        gain_parts[layer_index] = jnp.stack([gain_one, gain_two])
        shift_parts[layer_index] = jnp.stack([shift_one, shift_two])
        bias_parts[layer_index] = jnp.stack([bias_one, bias_two])
        collected[layer_index] = (
            lax.psum_scatter(triple_grad, "dp", scatter_dimension=0, tiled=True),
            lax.psum_scatter(exit_grad, "dp", scatter_dimension=1, tiled=True),
            lax.psum_scatter(expand_grad, "dp", scatter_dimension=0, tiled=True),
            lax.psum_scatter(shrink_grad, "dp", scatter_dimension=1, tiled=True),
        )
    stacked = [
        jnp.stack([collected[layer_index][member] for layer_index in range(LAYERS)])
        for member in range(4)
    ]
    triple_total, exit_total, expand_total, shrink_total = stacked
    gain_total, shift_total, bias_total = lax.psum(
        (jnp.stack(gain_parts), jnp.stack(shift_parts), jnp.stack(bias_parts)), ("dp", "tensor")
    )
    triple_bias_total, expand_bias_total = lax.psum(
        (jnp.stack(triple_bias_parts), jnp.stack(expand_bias_parts)), "dp"
    )
    return (
        mixed,
        upstream,
        triple_total,
        triple_bias_total,
        exit_total,
        expand_total,
        expand_bias_total,
        shrink_total,
        gain_total,
        shift_total,
        bias_total,
    )


def solution(mesh):
    return jax.shard_map(
        shards,
        mesh=mesh,
        in_specs=(
            P("tensor", "dp", None),
            P("tensor", "dp", None),
            P("dp"),
            P(None, "dp", None),
            P(None, "dp", None, "tensor"),
            P(None, None, "tensor"),
            P(None, "tensor", "dp"),
            P(None, "dp", "tensor"),
            P(None, "tensor"),
            P(None, "tensor", "dp"),
            P(),
            P(),
            P(),
        ),
        out_specs=(
            P("tensor", "dp", None),
            P("tensor", "dp", None),
            P(None, "dp", None, "tensor"),
            P(None, None, "tensor"),
            P(None, "tensor", "dp"),
            P(None, "dp", "tensor"),
            P(None, "tensor"),
            P(None, "tensor", "dp"),
            P(),
            P(),
            P(),
        ),
        check_vma=False,
    )
```

profile of v0, /device:TPU:0, one launch (start us, length us, event | category | flops | bytes accessed | tf_op | source)
XLA Modules:
  0.0 1529.0 jit_solution(13057020448451312139)
XLA Ops:
  39.7 48.1 %all-gather.23.cloned.1.call-done = bf16[1024,1,1024]{2,0,1:T(8,128)(2,1)} async-done(((bf16[256,1,1024]{2,0,1:T(8,128)(2,1)}), bf16[1024,1,1024]{2,0,1:T(8,128)(2,1)}) %all-gather.23.cloned.1.call-update) | async-done | bytes 2097168 | tf_op jit(solution)/shard_map/all_gather | solution.py:173
  110.9 28.1 %while.107 = (s32[]{:T(128)}, bf16[4,1024,64]{1,2,0:T(8,128)(2,1)}, f32[4,1024]{1,0:T(4,128)}, bf16[4,1024,64]{2,1,0:T(8,128)(2,1)S(1)}, bf16[4,1024,64]{2,1,0:T...) while((s32[]{:T(128)}, bf16[4,1024,64]{1,2,0:T(8,128)(2,1)}, ...), condition=%wide.region_7.8_spmd, body=%wide.region_2.7_spmd.sunk | while | flops 138968576 | bytes 8622382 | solution.py:96
  145.6 40.1 %reduce-scatter.17.cloned.1.call-done = bf16[256,1,1024]{2,0,1:T(8,128)(2,1)} async-done(((bf16[1024,1,1024]{2,0,1:T(8,128)(2,1)}), bf16[256,1,1024]{2,0,1:T(8,128)(2,1)}) %reduce-scatter.17.cloned.1.call-update) | async-done | bytes 524304 | tf_op jit(solution)/shard_map/reduce_scatter | solution.py:183
  215.5 48.0 %all-gather.25.cloned.1.call-done = bf16[1024,1,1024]{2,0,1:T(8,128)(2,1)} async-done(((bf16[256,1,1024]{2,0,1:T(8,128)(2,1)}), bf16[1024,1,1024]{2,0,1:T(8,128)(2,1)}) %all-gather.25.cloned.1.call-update) | async-done | bytes 2097168 | tf_op jit(solution)/shard_map/all_gather | solution.py:173
  299.9 43.1 %reduce-scatter.19.cloned.1.call-done = bf16[256,1,1024]{2,0,1:T(8,128)(2,1)} async-done(((bf16[1024,1,1024]{2,0,1:T(8,128)(2,1)}), bf16[256,1,1024]{2,0,1:T(8,128)(2,1)}) %reduce-scatter.19.cloned.1.call-update) | async-done | bytes 524304 | tf_op jit(solution)/shard_map/reduce_scatter | solution.py:183
  370.6 48.1 %all-gather.27.cloned.1.call-done = bf16[1024,1,1024]{2,0,1:T(8,128)(2,1)} async-done(((bf16[256,1,1024]{2,0,1:T(8,128)(2,1)}), bf16[1024,1,1024]{2,0,1:T(8,128)(2,1)}) %all-gather.27.cloned.1.call-update) | async-done | bytes 2097168 | tf_op jit(solution)/shard_map/all_gather | solution.py:173
  467.6 42.0 %reduce-scatter.21.cloned.1.call-done = bf16[256,1,1024]{2,0,1:T(8,128)(2,1)} async-done(((bf16[1024,1,1024]{2,0,1:T(8,128)(2,1)}), bf16[256,1,1024]{2,0,1:T(8,128)(2,1)}) %reduce-scatter.21.cloned.1.call-update) | async-done | bytes 524304 | tf_op jit(solution)/shard_map/reduce_scatter | solution.py:183
  539.4 48.0 %all-gather.29.cloned.1.call-done = bf16[1024,1,1024]{2,0,1:T(8,128)(2,1)} async-done(((bf16[256,1,1024]{2,0,1:T(8,128)(2,1)}), bf16[1024,1,1024]{2,0,1:T(8,128)(2,1)}) %all-gather.29.cloned.1.call-update) | async-done | bytes 2097168 | tf_op jit(solution)/shard_map/all_gather | solution.py:173
  602.0 31.7 %all-gather.31.cloned.1.call-done = bf16[1024,1,1024]{2,0,1:T(8,128)(2,1)} async-done(((bf16[256,1,1024]{2,0,1:T(8,128)(2,1)}), bf16[1024,1,1024]{2,0,1:T(8,128)(2,1)}) %all-gather.31.cloned.1.call-update) | async-done | bytes 2097168 | tf_op jit(solution)/shard_map/all_gather | solution.py:176
  633.7 28.9 %all-gather.49.cloned.1.call-done = bf16[1,1024,1024]{2,1,0:T(8,128)(2,1)} async-done(((bf16[1,1024,128]{2,1,0:T(8,128)(2,1)}), bf16[1,1024,1024]{2,1,0:T(8,128)(2,1)}) %all-gather.49.cloned.1.call-update) | async-done | bytes 2097168 | tf_op jit(solution)/shard_map/all_gather | solution.py:209
  680.9 38.0 %reduce-scatter.25.cloned.1.call-done = bf16[256,1,1024]{2,0,1:T(8,128)(2,1)} async-done(((bf16[1024,1,1024]{2,0,1:T(8,128)(2,1)}), bf16[256,1,1024]{2,0,1:T(8,128)(2,1)}) %reduce-scatter.25.cloned.1.call-update) | async-done | bytes 524304 | tf_op jit(solution)/shard_map/reduce_scatter | solution.py:195
  721.0 43.2 %reduce-scatter.23.cloned.1.call-done = bf16[256,1,1024]{2,0,1:T(8,128)(2,1)} async-done(((bf16[1024,1,1024]{2,0,1:T(8,128)(2,1)}), bf16[256,1,1024]{2,0,1:T(8,128)(2,1)}) %reduce-scatter.23.cloned.1.call-update) | async-done | bytes 524304 | tf_op jit(solution)/shard_map/reduce_scatter | solution.py:183
  770.0 43.6 %all-gather.33.cloned.1.call-done = bf16[1024,1,1024]{2,0,1:T(8,128)(2,1)} async-done(((bf16[256,1,1024]{2,0,1:T(8,128)(2,1)}), bf16[1024,1,1024]{2,0,1:T(8,128)(2,1)}) %all-gather.33.cloned.1.call-update) | async-done | bytes 2097168 | tf_op jit(solution)/shard_map/all_gather | solution.py:176
  818.6 45.1 %while.111 = (s32[]{:T(128)}, f32[4,1024,64]{1,2,0:T(8,128)}, f32[4,1024,64]{1,2,0:T(8,128)S(1)}, bf16[4,1024,64]{1,2,0:T(8,128)(2,1)S(1)}, bf16[4,1024,64]{2,1,...) while((s32[]{:T(128)}, f32[4,1024,64]{1,2,0:T(8,128)}, ...), condition=%wide.region_31.32_spmd, body=%wide.region_27.31_spmd.sunk | while | flops 340098560 | bytes 21916056 | solution.py:147
  878.1 42.7 %reduce-scatter.27.cloned.1.call-done = bf16[256,1,1024]{2,0,1:T(8,128)(2,1)} async-done(((bf16[1024,1,1024]{2,0,1:T(8,128)(2,1)}), bf16[256,1,1024]{2,0,1:T(8,128)(2,1)}) %reduce-scatter.27.cloned.1.call-update) | async-done | bytes 524304 | tf_op jit(solution)/shard_map/reduce_scatter | solution.py:195
  926.3 45.0 %all-gather.35.cloned.1.call-done = bf16[1024,1,1024]{2,0,1:T(8,128)(2,1)} async-done(((bf16[256,1,1024]{2,0,1:T(8,128)(2,1)}), bf16[1024,1,1024]{2,0,1:T(8,128)(2,1)}) %all-gather.35.cloned.1.call-update) | async-done | bytes 2097168 | tf_op jit(solution)/shard_map/all_gather | solution.py:176
  983.7 42.7 %reduce-scatter.29.cloned.1.call-done = bf16[256,1,1024]{2,0,1:T(8,128)(2,1)} async-done(((bf16[1024,1,1024]{2,0,1:T(8,128)(2,1)}), bf16[256,1,1024]{2,0,1:T(8,128)(2,1)}) %reduce-scatter.29.cloned.1.call-update) | async-done | bytes 524304 | tf_op jit(solution)/shard_map/reduce_scatter | solution.py:195
  1085.8 45.2 %while.113 = (s32[]{:T(128)}, f32[4,1024,64]{1,2,0:T(8,128)}, f32[4,1024,64]{1,2,0:T(8,128)S(1)}, bf16[4,1024,64]{1,2,0:T(8,128)(2,1)S(1)}, bf16[4,1024,64]{2,1,...) while((s32[]{:T(128)}, f32[4,1024,64]{1,2,0:T(8,128)}, ...), condition=%wide.region_42.43_spmd, body=%wide.region_38.42_spmd.sunk | while | flops 340098560 | bytes 21916056 | solution.py:147
  1188.3 52.6 %reduce-scatter.43.cloned.1.call-done = f32[128,1024]{1,0:T(8,128)} async-done(((f32[1024,1024]{1,0:T(8,128)}), f32[128,1024]{1,0:T(8,128)}) %reduce-scatter.43.cloned.1.call-update) | async-done | bytes 524304 | tf_op jit(solution)/shard_map/reduce_scatter | solution.py:337
  1240.9 54.7 %reduce-scatter.41.cloned.1.call-done = f32[128,1024]{1,0:T(8,128)} async-done(((f32[1024,1024]{1,0:T(8,128)}), f32[128,1024]{1,0:T(8,128)}) %reduce-scatter.41.cloned.1.call-update) | async-done | bytes 524304 | tf_op jit(solution)/shard_map/reduce_scatter | solution.py:337
  1335.0 39.4 %reduce-scatter.37.cloned.1.call-done = f32[256,128]{1,0:T(8,128)} async-done(((f32[256,1024]{1,0:T(8,128)}), f32[256,128]{1,0:T(8,128)}) %reduce-scatter.37.cloned.1.call-update) | async-done | bytes 131088 | tf_op jit(solution)/shard_map/reduce_scatter | solution.py:336
  1376.1 44.6 %reduce-scatter.31.cloned.1.call-done = bf16[256,1,1024]{2,0,1:T(8,128)(2,1)} async-done(((bf16[1024,1,1024]{2,0,1:T(8,128)(2,1)}), bf16[256,1,1024]{2,0,1:T(8,128)(2,1)}) %reduce-scatter.31.cloned.1.call-update) | async-done | bytes 524304 | tf_op jit(solution)/shard_map/reduce_scatter | solution.py:195
  1426.0 40.6 %all-reduce = (f32[2,2,1024]{2,1,0:T(2,128)}, f32[2,2,1024]{2,1,0:T(2,128)}, f32[2,2,1024]{2,1,0:T(2,128)}) all-reduce(f32[2,2,1024]{2,1,0:T(2,128)S(1)} %pad_maximum_fusion.10, f32[2,2,1024]{2,1,0:T(2,128)S(1)} %pad_maximum_fusion.11, f32[2,2,1024]{2,1,0:T(2,128)S(1)} %pad_maximum_fusion.12), channel_id=1, replica_groups=mesh['dp'=8,'tensor'=4] {'dp','tensor'}, use_global_device_ids=true, to_apply=%region_64.65 | all-reduce | flops 12288 | bytes 98304 | tf_op jit(solution)/shard_map/psum | solution.py:345
  1470.0 49.8 %reduce-scatter.33.cloned.1.call-done = f32[128,3,256]{2,0,1:T(8,128)} async-done(((f32[1024,3,256]{2,0,1:T(8,128)}), f32[128,3,256]{2,0,1:T(8,128)}) %reduce-scatter.33.cloned.1.call-update) | async-done | bytes 393232 | tf_op jit(solution)/shard_map/reduce_scatter | solution.py:335
  (839 shorter events, 692.9 us)
Async XLA Ops:
  17.3 168.5 %reduce-scatter.17.cloned.1.call-start = ((), (), s32[]{:S(2)}) async-start(), calls=%async_computation.17 | async-start | bytes 2621440 | tf_op jit(solution)/shard_map/reduce_scatter | solution.py:183
  144.9 118.6 %all-gather.25.cloned.1.call-start = ((), (), s32[]{:S(2)}) async-start(), calls=%async_computation.18 | async-start | bytes 2621440 | tf_op jit(solution)/shard_map/all_gather | solution.py:173
  190.6 102.3 %all-gather.43.cloned.1.call-start = ((), (), s32[]{:S(2)}) async-start(), calls=%async_computation.42 | async-start | bytes 2359296 | tf_op jit(solution)/shard_map/all_gather | solution.py:209
  192.6 150.4 %reduce-scatter.19.cloned.1.call-start = ((), (), s32[]{:S(2)}) async-start(), calls=%async_computation.19 | async-start | bytes 2621440 | tf_op jit(solution)/shard_map/reduce_scatter | solution.py:183
  299.8 118.9 %all-gather.27.cloned.1.call-start = ((), (), s32[]{:S(2)}) async-start(), calls=%async_computation.20 | async-start | bytes 2621440 | tf_op jit(solution)/shard_map/all_gather | solution.py:173
  345.7 163.8 %reduce-scatter.21.cloned.1.call-start = ((), (), s32[]{:S(2)}) async-start(), calls=%async_computation.21 | async-start | bytes 2621440 | tf_op jit(solution)/shard_map/reduce_scatter | solution.py:183
  467.5 119.9 %all-gather.29.cloned.1.call-start = ((), (), s32[]{:S(2)}) async-start(), calls=%async_computation.22 | async-start | bytes 2621440 | tf_op jit(solution)/shard_map/all_gather | solution.py:173
  512.2 121.5 %all-gather.31.cloned.1.call-start = ((), (), s32[]{:S(2)}) async-start(), calls=%async_computation.24 | async-start | bytes 2621440 | tf_op jit(solution)/shard_map/all_gather | solution.py:176
  514.4 148.2 %all-gather.49.cloned.1.call-start = ((), (), s32[]{:S(2)}) async-start(), calls=%async_computation.45 | async-start | bytes 2359296 | tf_op jit(solution)/shard_map/all_gather | solution.py:209
  515.0 203.9 %reduce-scatter.25.cloned.1.call-start = ((), (), s32[]{:S(2)}) async-start(), calls=%async_computation.25 | async-start | bytes 2621440 | tf_op jit(solution)/shard_map/reduce_scatter | solution.py:195
  680.8 132.8 %all-gather.33.cloned.1.call-start = ((), (), s32[]{:S(2)}) async-start(), calls=%async_computation.26 | async-start | bytes 2621440 | tf_op jit(solution)/shard_map/all_gather | solution.py:176
  768.3 152.5 %reduce-scatter.27.cloned.1.call-start = ((), (), s32[]{:S(2)}) async-start(), calls=%async_computation.27 | async-start | bytes 2621440 | tf_op jit(solution)/shard_map/reduce_scatter | solution.py:195
  878.0 93.2 %all-gather.35.cloned.1.call-start = ((), (), s32[]{:S(2)}) async-start(), calls=%async_computation.28 | async-start | bytes 2621440 | tf_op jit(solution)/shard_map/all_gather | solution.py:176
  925.8 100.6 %reduce-scatter.29.cloned.1.call-start = ((), (), s32[]{:S(2)}) async-start(), calls=%async_computation.29 | async-start | bytes 2621440 | tf_op jit(solution)/shard_map/reduce_scatter | solution.py:195
  983.7 93.8 %all-gather.37.cloned.1.call-start = ((), (), s32[]{:S(2)}) async-start(), calls=%async_computation.30 | async-start | bytes 2621440 | tf_op jit(solution)/shard_map/all_gather | solution.py:176
  1032.0 129.2 %reduce-scatter.47.cloned.1.call-start = ((), (), s32[]{:S(2)}) async-start(), calls=%async_computation.39 | async-start | bytes 4718592 | tf_op jit(solution)/shard_map/reduce_scatter | solution.py:338
  1038.7 147.2 %reduce-scatter.45.cloned.1.call-start = ((), (), s32[]{:S(2)}) async-start(), calls=%async_computation.38 | async-start | bytes 4718592 | tf_op jit(solution)/shard_map/reduce_scatter | solution.py:338
  1046.4 194.5 %reduce-scatter.43.cloned.1.call-start = ((), (), s32[]{:S(2)}) async-start(), calls=%async_computation.37 | async-start | bytes 4718592 | tf_op jit(solution)/shard_map/reduce_scatter | solution.py:337
  1054.1 241.5 %reduce-scatter.41.cloned.1.call-start = ((), (), s32[]{:S(2)}) async-start(), calls=%async_computation.36 | async-start | bytes 4718592 | tf_op jit(solution)/shard_map/reduce_scatter | solution.py:337
  1061.6 273.4 %reduce-scatter.39.cloned.1.call-start = ((), (), s32[]{:S(2)}) async-start(), calls=%async_computation.35 | async-start | bytes 1179648 | tf_op jit(solution)/shard_map/reduce_scatter | solution.py:336
  1065.1 309.4 %reduce-scatter.37.cloned.1.call-start = ((), (), s32[]{:S(2)}) async-start(), calls=%async_computation.34 | async-start | bytes 1179648 | tf_op jit(solution)/shard_map/reduce_scatter | solution.py:336
  1084.5 336.2 %reduce-scatter.31.cloned.1.call-start = ((), (), s32[]{:S(2)}) async-start(), calls=%async_computation.31 | async-start | bytes 2621440 | tf_op jit(solution)/shard_map/reduce_scatter | solution.py:195
  1145.1 324.9 %reduce-scatter.35.cloned.1.call-start = ((), (), s32[]{:S(2)}) async-start(), calls=%async_computation.33 | async-start | bytes 3538944 | tf_op jit(solution)/shard_map/reduce_scatter | solution.py:335
  1150.7 369.1 %reduce-scatter.33.cloned.1.call-start = ((), (), s32[]{:S(2)}) async-start(), calls=%async_computation.32 | async-start | bytes 3538944 | tf_op jit(solution)/shard_map/reduce_scatter | solution.py:335
  (119 other events, 6083.2 us)
Sparse Core Ops, SparseCore 0:
  41.8 45.9 all-gather.22
  143.1 42.5 reduce-scatter.16
  217.5 45.9 all-gather.24
  299.0 43.8 reduce-scatter.18
  372.8 45.9 all-gather.26
  466.9 42.5 reduce-scatter.20
  541.5 45.9 all-gather.28
  589.1 44.5 all-gather.30
  675.0 43.8 reduce-scatter.24
  721.0 43.1 reduce-scatter.22
  768.4 45.2 all-gather.32
  878.2 42.5 reduce-scatter.26
  926.0 45.2 all-gather.34
  983.8 42.5 reduce-scatter.28
  1032.1 45.2 all-gather.36
  1081.1 50.0 reduce-scatter.46
  1134.6 51.2 reduce-scatter.44
  1189.5 51.3 reduce-scatter.42
  1244.3 51.2 reduce-scatter.40
  1298.9 36.0 reduce-scatter.38
  1338.4 36.0 reduce-scatter.36
  1376.8 43.8 reduce-scatter.30
  1424.1 45.8 reduce-scatter.34
  1473.6 46.1 reduce-scatter.32
  (6 shorter events, 162.3 us)
where the time goes:
time: 1540 us; the launch traced here: 1530 us
  waiting for transfers between devices  1010 us (66%)
  matrix products  190 us (12%)
  local copies, waits for them, and re-layouts  148 us (10%)
  blocking collectives  89.3 us (6%)
  other arithmetic  69.1 us (4%)
  between operations  16.8 us (1%)
    all_gather x4, waiting for transfers between devices, spread_rows(): return lax.all_gather(normed, 'tensor', axis=0, tiled=True)  192 us
    reduce_scatter x4, waiting for transfers between devices, collect_rows(): lax.psum_scatter(partial_term(jnp.int32(0), row_count * lax.axis_size('te...  168 us
    reduce_scatter x4, waiting for transfers between devices, collect_grads(): lax.psum_scatter(partial_term(jnp.int32(0), row_count * lax.axis_size('te...  168 us
    all_gather x4, waiting for transfers between devices, spread_grads(): return lax.all_gather(upstream_low, 'tensor', axis=0, tiled=True)  133 us
    reduce_scatter x2, waiting for transfers between devices, shards(): lax.psum_scatter(expand_grad, 'dp', scatter_dimension=0, tiled=True)  107 us
    reduce_scatter x2, waiting for transfers between devices, shards(): lax.psum_scatter(triple_grad, 'dp', scatter_dimension=0, tiled=True)  53.3 us
    reduce_scatter x2, waiting for transfers between devices, shards(): lax.psum_scatter(exit_grad, 'dp', scatter_dimension=1, tiled=True)  52.6 us
    all_gather x2, waiting for transfers between devices, shards(): lax.all_gather(expand_weight[layer_index], 'dp', axis=0, tiled=True)  46.1 us
  transfers between devices with their start and end apart: 30, of which 29 were waited for; matrix products, arithmetic and copies ran while one was open for 12% of the time, Pallas kernels for 0%

commit v1 on v0

--- a/solution.py
+++ b/solution.py
@@ -342,8 +342,9 @@
         for member in range(4)
     ]
     triple_total, exit_total, expand_total, shrink_total = stacked
-    gain_total, shift_total, bias_total = lax.psum(
-        (jnp.stack(gain_parts), jnp.stack(shift_parts), jnp.stack(bias_parts)), ("dp", "tensor")
+    note_the_tables = lambda inp: lax.psum(lax.psum(inp, "tensor"), "dp")
+    gain_total, shift_total, bias_total = note_the_tables(
+        (jnp.stack(gain_parts), jnp.stack(shift_parts), jnp.stack(bias_parts))
     )
     triple_bias_total, expand_bias_total = lax.psum(
         (jnp.stack(triple_bias_parts), jnp.stack(expand_bias_parts)), "dp"

time: 1540 us -> 1540 us (level)
  blocking collectives: 89.3 us -> 67.4 us
  waiting for transfers between devices: 1010 us -> 1030 us
    reduce_scatter x2, waiting for transfers between devices: 52.6 us -> 76.3 us  [shards(): lax.psum_scatter(exit_grad, 'dp', scatter_dimension=1, tiled=True)]
    psum x1, blocking collectives: 40.6 us -> 17.6 us  [shards(): note_the_tables = lambda inp: lax.psum(lax.psum(inp, 'tensor'), 'dp')]
where the time goes in v1:
time: 1540 us; the launch traced here: 1530 us
  waiting for transfers between devices  1030 us (67%)
  matrix products  190 us (12%)
  local copies, waits for them, and re-layouts  148 us (10%)
  other arithmetic  69.1 us (4%)
  blocking collectives  67.4 us (4%)
  between operations  16.8 us (1%)
    all_gather x4, waiting for transfers between devices, spread_rows(): return lax.all_gather(normed, 'tensor', axis=0, tiled=True)  192 us
    reduce_scatter x4, waiting for transfers between devices, collect_rows(): lax.psum_scatter(partial_term(jnp.int32(0), row_count * lax.axis_size('te...  168 us
    reduce_scatter x4, waiting for transfers between devices, collect_grads(): lax.psum_scatter(partial_term(jnp.int32(0), row_count * lax.axis_size('te...  168 us
    all_gather x4, waiting for transfers between devices, spread_grads(): return lax.all_gather(upstream_low, 'tensor', axis=0, tiled=True)  133 us
    reduce_scatter x2, waiting for transfers between devices, shards(): lax.psum_scatter(expand_grad, 'dp', scatter_dimension=0, tiled=True)  107 us
    reduce_scatter x2, waiting for transfers between devices, shards(): lax.psum_scatter(exit_grad, 'dp', scatter_dimension=1, tiled=True)  76.3 us
    reduce_scatter x2, waiting for transfers between devices, shards(): lax.psum_scatter(triple_grad, 'dp', scatter_dimension=0, tiled=True)  51.8 us
    all_gather x2, waiting for transfers between devices, shards(): lax.all_gather(expand_weight[layer_index], 'dp', axis=0, tiled=True)  46.1 us
  transfers between devices with their start and end apart: 30, of which 29 were waited for; matrix products, arithmetic and copies ran while one was open for 12% of the time, Pallas kernels for 0%

profile of v1, /device:TPU:0, one launch (start us, length us, event | category | flops | bytes accessed | tf_op | source)
XLA Modules:
  0.0 1529.2 jit_solution(1203030126719709577)
XLA Ops:
  39.7 48.1 %all-gather.23.cloned.1.call-done = bf16[1024,1,1024]{2,0,1:T(8,128)(2,1)} async-done(((bf16[256,1,1024]{2,0,1:T(8,128)(2,1)}), bf16[1024,1,1024]{2,0,1:T(8,128)(2,1)}) %all-gather.23.cloned.1.call-update) | async-done | bytes 2097168 | tf_op jit(solution)/shard_map/all_gather | solution.py:173
  110.9 28.1 %while.107 = (s32[]{:T(128)}, bf16[4,1024,64]{1,2,0:T(8,128)(2,1)}, f32[4,1024]{1,0:T(4,128)}, bf16[4,1024,64]{2,1,0:T(8,128)(2,1)S(1)}, bf16[4,1024,64]{2,1,0:T...) while((s32[]{:T(128)}, bf16[4,1024,64]{1,2,0:T(8,128)(2,1)}, ...), condition=%wide.region_7.8_spmd, body=%wide.region_2.7_spmd.sunk | while | flops 138968576 | bytes 8622382 | solution.py:96
  145.6 40.1 %reduce-scatter.17.cloned.1.call-done = bf16[256,1,1024]{2,0,1:T(8,128)(2,1)} async-done(((bf16[1024,1,1024]{2,0,1:T(8,128)(2,1)}), bf16[256,1,1024]{2,0,1:T(8,128)(2,1)}) %reduce-scatter.17.cloned.1.call-update) | async-done | bytes 524304 | tf_op jit(solution)/shard_map/reduce_scatter | solution.py:183
  215.5 48.0 %all-gather.25.cloned.1.call-done = bf16[1024,1,1024]{2,0,1:T(8,128)(2,1)} async-done(((bf16[256,1,1024]{2,0,1:T(8,128)(2,1)}), bf16[1024,1,1024]{2,0,1:T(8,128)(2,1)}) %all-gather.25.cloned.1.call-update) | async-done | bytes 2097168 | tf_op jit(solution)/shard_map/all_gather | solution.py:173
  299.9 43.1 %reduce-scatter.19.cloned.1.call-done = bf16[256,1,1024]{2,0,1:T(8,128)(2,1)} async-done(((bf16[1024,1,1024]{2,0,1:T(8,128)(2,1)}), bf16[256,1,1024]{2,0,1:T(8,128)(2,1)}) %reduce-scatter.19.cloned.1.call-update) | async-done | bytes 524304 | tf_op jit(solution)/shard_map/reduce_scatter | solution.py:183
  370.6 48.1 %all-gather.27.cloned.1.call-done = bf16[1024,1,1024]{2,0,1:T(8,128)(2,1)} async-done(((bf16[256,1,1024]{2,0,1:T(8,128)(2,1)}), bf16[1024,1,1024]{2,0,1:T(8,128)(2,1)}) %all-gather.27.cloned.1.call-update) | async-done | bytes 2097168 | tf_op jit(solution)/shard_map/all_gather | solution.py:173
  467.6 42.0 %reduce-scatter.21.cloned.1.call-done = bf16[256,1,1024]{2,0,1:T(8,128)(2,1)} async-done(((bf16[1024,1,1024]{2,0,1:T(8,128)(2,1)}), bf16[256,1,1024]{2,0,1:T(8,128)(2,1)}) %reduce-scatter.21.cloned.1.call-update) | async-done | bytes 524304 | tf_op jit(solution)/shard_map/reduce_scatter | solution.py:183
  539.4 48.0 %all-gather.29.cloned.1.call-done = bf16[1024,1,1024]{2,0,1:T(8,128)(2,1)} async-done(((bf16[256,1,1024]{2,0,1:T(8,128)(2,1)}), bf16[1024,1,1024]{2,0,1:T(8,128)(2,1)}) %all-gather.29.cloned.1.call-update) | async-done | bytes 2097168 | tf_op jit(solution)/shard_map/all_gather | solution.py:173
  602.0 31.7 %all-gather.31.cloned.1.call-done = bf16[1024,1,1024]{2,0,1:T(8,128)(2,1)} async-done(((bf16[256,1,1024]{2,0,1:T(8,128)(2,1)}), bf16[1024,1,1024]{2,0,1:T(8,128)(2,1)}) %all-gather.31.cloned.1.call-update) | async-done | bytes 2097168 | tf_op jit(solution)/shard_map/all_gather | solution.py:176
  633.7 28.9 %all-gather.49.cloned.1.call-done = bf16[1,1024,1024]{2,1,0:T(8,128)(2,1)} async-done(((bf16[1,1024,128]{2,1,0:T(8,128)(2,1)}), bf16[1,1024,1024]{2,1,0:T(8,128)(2,1)}) %all-gather.49.cloned.1.call-update) | async-done | bytes 2097168 | tf_op jit(solution)/shard_map/all_gather | solution.py:209
  680.9 38.0 %reduce-scatter.25.cloned.1.call-done = bf16[256,1,1024]{2,0,1:T(8,128)(2,1)} async-done(((bf16[1024,1,1024]{2,0,1:T(8,128)(2,1)}), bf16[256,1,1024]{2,0,1:T(8,128)(2,1)}) %reduce-scatter.25.cloned.1.call-update) | async-done | bytes 524304 | tf_op jit(solution)/shard_map/reduce_scatter | solution.py:195
  721.0 43.2 %reduce-scatter.23.cloned.1.call-done = bf16[256,1,1024]{2,0,1:T(8,128)(2,1)} async-done(((bf16[1024,1,1024]{2,0,1:T(8,128)(2,1)}), bf16[256,1,1024]{2,0,1:T(8,128)(2,1)}) %reduce-scatter.23.cloned.1.call-update) | async-done | bytes 524304 | tf_op jit(solution)/shard_map/reduce_scatter | solution.py:183
  770.0 43.6 %all-gather.33.cloned.1.call-done = bf16[1024,1,1024]{2,0,1:T(8,128)(2,1)} async-done(((bf16[256,1,1024]{2,0,1:T(8,128)(2,1)}), bf16[1024,1,1024]{2,0,1:T(8,128)(2,1)}) %all-gather.33.cloned.1.call-update) | async-done | bytes 2097168 | tf_op jit(solution)/shard_map/all_gather | solution.py:176
  818.6 45.1 %while.111 = (s32[]{:T(128)}, f32[4,1024,64]{1,2,0:T(8,128)}, f32[4,1024,64]{1,2,0:T(8,128)S(1)}, bf16[4,1024,64]{1,2,0:T(8,128)(2,1)S(1)}, bf16[4,1024,64]{2,1,...) while((s32[]{:T(128)}, f32[4,1024,64]{1,2,0:T(8,128)}, ...), condition=%wide.region_31.32_spmd, body=%wide.region_27.31_spmd.sunk | while | flops 340098560 | bytes 21916056 | solution.py:147
  878.1 42.7 %reduce-scatter.27.cloned.1.call-done = bf16[256,1,1024]{2,0,1:T(8,128)(2,1)} async-done(((bf16[1024,1,1024]{2,0,1:T(8,128)(2,1)}), bf16[256,1,1024]{2,0,1:T(8,128)(2,1)}) %reduce-scatter.27.cloned.1.call-update) | async-done | bytes 524304 | tf_op jit(solution)/shard_map/reduce_scatter | solution.py:195
  926.3 45.0 %all-gather.35.cloned.1.call-done = bf16[1024,1,1024]{2,0,1:T(8,128)(2,1)} async-done(((bf16[256,1,1024]{2,0,1:T(8,128)(2,1)}), bf16[1024,1,1024]{2,0,1:T(8,128)(2,1)}) %all-gather.35.cloned.1.call-update) | async-done | bytes 2097168 | tf_op jit(solution)/shard_map/all_gather | solution.py:176
  983.7 42.7 %reduce-scatter.29.cloned.1.call-done = bf16[256,1,1024]{2,0,1:T(8,128)(2,1)} async-done(((bf16[1024,1,1024]{2,0,1:T(8,128)(2,1)}), bf16[256,1,1024]{2,0,1:T(8,128)(2,1)}) %reduce-scatter.29.cloned.1.call-update) | async-done | bytes 524304 | tf_op jit(solution)/shard_map/reduce_scatter | solution.py:195
  1085.8 45.2 %while.113 = (s32[]{:T(128)}, f32[4,1024,64]{1,2,0:T(8,128)}, f32[4,1024,64]{1,2,0:T(8,128)S(1)}, bf16[4,1024,64]{1,2,0:T(8,128)(2,1)S(1)}, bf16[4,1024,64]{2,1,...) while((s32[]{:T(128)}, f32[4,1024,64]{1,2,0:T(8,128)}, ...), condition=%wide.region_42.43_spmd, body=%wide.region_38.42_spmd.sunk | while | flops 340098560 | bytes 21916056 | solution.py:147
  1188.3 52.6 %reduce-scatter.43.cloned.1.call-done = f32[128,1024]{1,0:T(8,128)} async-done(((f32[1024,1024]{1,0:T(8,128)}), f32[128,1024]{1,0:T(8,128)}) %reduce-scatter.43.cloned.1.call-update) | async-done | bytes 524304 | tf_op jit(solution)/shard_map/reduce_scatter | solution.py:337
  1240.9 54.7 %reduce-scatter.41.cloned.1.call-done = f32[128,1024]{1,0:T(8,128)} async-done(((f32[1024,1024]{1,0:T(8,128)}), f32[128,1024]{1,0:T(8,128)}) %reduce-scatter.41.cloned.1.call-update) | async-done | bytes 524304 | tf_op jit(solution)/shard_map/reduce_scatter | solution.py:337
  1298.2 36.9 %reduce-scatter.39.cloned.1.call-done = f32[256,128]{1,0:T(8,128)} async-done(((f32[256,1024]{1,0:T(8,128)}), f32[256,128]{1,0:T(8,128)}) %reduce-scatter.39.cloned.1.call-update) | async-done | bytes 131088 | tf_op jit(solution)/shard_map/reduce_scatter | solution.py:336
  1335.0 39.4 %reduce-scatter.37.cloned.1.call-done = f32[256,128]{1,0:T(8,128)} async-done(((f32[256,1024]{1,0:T(8,128)}), f32[256,128]{1,0:T(8,128)}) %reduce-scatter.37.cloned.1.call-update) | async-done | bytes 131088 | tf_op jit(solution)/shard_map/reduce_scatter | solution.py:336
  1376.1 44.6 %reduce-scatter.31.cloned.1.call-done = bf16[256,1,1024]{2,0,1:T(8,128)(2,1)} async-done(((bf16[1024,1,1024]{2,0,1:T(8,128)(2,1)}), bf16[256,1,1024]{2,0,1:T(8,128)(2,1)}) %reduce-scatter.31.cloned.1.call-update) | async-done | bytes 524304 | tf_op jit(solution)/shard_map/reduce_scatter | solution.py:195
  1470.2 49.8 %reduce-scatter.33.cloned.1.call-done = f32[128,3,256]{2,0,1:T(8,128)} async-done(((f32[1024,3,256]{2,0,1:T(8,128)}), f32[128,3,256]{2,0,1:T(8,128)}) %reduce-scatter.33.cloned.1.call-update) | async-done | bytes 393232 | tf_op jit(solution)/shard_map/reduce_scatter | solution.py:335
  (839 shorter events, 696.9 us)
Async XLA Ops:
  17.3 168.5 %reduce-scatter.17.cloned.1.call-start = ((), (), s32[]{:S(2)}) async-start(), calls=%async_computation.17 | async-start | bytes 2621440 | tf_op jit(solution)/shard_map/reduce_scatter | solution.py:183
  144.9 118.6 %all-gather.25.cloned.1.call-start = ((), (), s32[]{:S(2)}) async-start(), calls=%async_computation.18 | async-start | bytes 2621440 | tf_op jit(solution)/shard_map/all_gather | solution.py:173
  190.6 102.3 %all-gather.43.cloned.1.call-start = ((), (), s32[]{:S(2)}) async-start(), calls=%async_computation.42 | async-start | bytes 2359296 | tf_op jit(solution)/shard_map/all_gather | solution.py:209
  192.6 150.4 %reduce-scatter.19.cloned.1.call-start = ((), (), s32[]{:S(2)}) async-start(), calls=%async_computation.19 | async-start | bytes 2621440 | tf_op jit(solution)/shard_map/reduce_scatter | solution.py:183
  299.8 118.9 %all-gather.27.cloned.1.call-start = ((), (), s32[]{:S(2)}) async-start(), calls=%async_computation.20 | async-start | bytes 2621440 | tf_op jit(solution)/shard_map/all_gather | solution.py:173
  345.7 163.8 %reduce-scatter.21.cloned.1.call-start = ((), (), s32[]{:S(2)}) async-start(), calls=%async_computation.21 | async-start | bytes 2621440 | tf_op jit(solution)/shard_map/reduce_scatter | solution.py:183
  467.5 119.9 %all-gather.29.cloned.1.call-start = ((), (), s32[]{:S(2)}) async-start(), calls=%async_computation.22 | async-start | bytes 2621440 | tf_op jit(solution)/shard_map/all_gather | solution.py:173
  512.2 121.5 %all-gather.31.cloned.1.call-start = ((), (), s32[]{:S(2)}) async-start(), calls=%async_computation.24 | async-start | bytes 2621440 | tf_op jit(solution)/shard_map/all_gather | solution.py:176
  514.4 148.2 %all-gather.49.cloned.1.call-start = ((), (), s32[]{:S(2)}) async-start(), calls=%async_computation.45 | async-start | bytes 2359296 | tf_op jit(solution)/shard_map/all_gather | solution.py:209
  515.0 203.9 %reduce-scatter.25.cloned.1.call-start = ((), (), s32[]{:S(2)}) async-start(), calls=%async_computation.25 | async-start | bytes 2621440 | tf_op jit(solution)/shard_map/reduce_scatter | solution.py:195
  680.8 132.8 %all-gather.33.cloned.1.call-start = ((), (), s32[]{:S(2)}) async-start(), calls=%async_computation.26 | async-start | bytes 2621440 | tf_op jit(solution)/shard_map/all_gather | solution.py:176
  768.3 152.5 %reduce-scatter.27.cloned.1.call-start = ((), (), s32[]{:S(2)}) async-start(), calls=%async_computation.27 | async-start | bytes 2621440 | tf_op jit(solution)/shard_map/reduce_scatter | solution.py:195
  878.0 93.2 %all-gather.35.cloned.1.call-start = ((), (), s32[]{:S(2)}) async-start(), calls=%async_computation.28 | async-start | bytes 2621440 | tf_op jit(solution)/shard_map/all_gather | solution.py:176
  925.8 100.6 %reduce-scatter.29.cloned.1.call-start = ((), (), s32[]{:S(2)}) async-start(), calls=%async_computation.29 | async-start | bytes 2621440 | tf_op jit(solution)/shard_map/reduce_scatter | solution.py:195
  983.7 93.8 %all-gather.37.cloned.1.call-start = ((), (), s32[]{:S(2)}) async-start(), calls=%async_computation.30 | async-start | bytes 2621440 | tf_op jit(solution)/shard_map/all_gather | solution.py:176
  1032.0 129.2 %reduce-scatter.47.cloned.1.call-start = ((), (), s32[]{:S(2)}) async-start(), calls=%async_computation.39 | async-start | bytes 4718592 | tf_op jit(solution)/shard_map/reduce_scatter | solution.py:338
  1038.7 147.2 %reduce-scatter.45.cloned.1.call-start = ((), (), s32[]{:S(2)}) async-start(), calls=%async_computation.38 | async-start | bytes 4718592 | tf_op jit(solution)/shard_map/reduce_scatter | solution.py:338
  1046.4 194.5 %reduce-scatter.43.cloned.1.call-start = ((), (), s32[]{:S(2)}) async-start(), calls=%async_computation.37 | async-start | bytes 4718592 | tf_op jit(solution)/shard_map/reduce_scatter | solution.py:337
  1054.1 241.5 %reduce-scatter.41.cloned.1.call-start = ((), (), s32[]{:S(2)}) async-start(), calls=%async_computation.36 | async-start | bytes 4718592 | tf_op jit(solution)/shard_map/reduce_scatter | solution.py:337
  1061.6 273.4 %reduce-scatter.39.cloned.1.call-start = ((), (), s32[]{:S(2)}) async-start(), calls=%async_computation.35 | async-start | bytes 1179648 | tf_op jit(solution)/shard_map/reduce_scatter | solution.py:336
  1065.1 309.4 %reduce-scatter.37.cloned.1.call-start = ((), (), s32[]{:S(2)}) async-start(), calls=%async_computation.34 | async-start | bytes 1179648 | tf_op jit(solution)/shard_map/reduce_scatter | solution.py:336
  1084.5 336.2 %reduce-scatter.31.cloned.1.call-start = ((), (), s32[]{:S(2)}) async-start(), calls=%async_computation.31 | async-start | bytes 2621440 | tf_op jit(solution)/shard_map/reduce_scatter | solution.py:195
  1145.1 325.1 %reduce-scatter.35.cloned.1.call-start = ((), (), s32[]{:S(2)}) async-start(), calls=%async_computation.33 | async-start | bytes 3538944 | tf_op jit(solution)/shard_map/reduce_scatter | solution.py:335
  1150.7 369.3 %reduce-scatter.33.cloned.1.call-start = ((), (), s32[]{:S(2)}) async-start(), calls=%async_computation.32 | async-start | bytes 3538944 | tf_op jit(solution)/shard_map/reduce_scatter | solution.py:335
  (119 other events, 6083.2 us)
Sparse Core Ops, SparseCore 0:
  41.8 45.9 all-gather.22
  143.1 42.5 reduce-scatter.16
  217.5 45.9 all-gather.24
  299.0 43.8 reduce-scatter.18
  372.8 45.9 all-gather.26
  466.9 42.5 reduce-scatter.20
  541.5 45.9 all-gather.28
  589.1 44.5 all-gather.30
  675.0 43.8 reduce-scatter.24
  721.0 43.1 reduce-scatter.22
  768.4 45.2 all-gather.32
  878.2 42.5 reduce-scatter.26
  926.0 45.2 all-gather.34
  983.8 42.5 reduce-scatter.28
  1032.1 45.2 all-gather.36
  1081.1 50.0 reduce-scatter.46
  1134.6 51.2 reduce-scatter.44
  1189.5 51.3 reduce-scatter.42
  1244.3 51.2 reduce-scatter.40
  1298.9 36.0 reduce-scatter.38
  1338.4 36.0 reduce-scatter.36
  1376.8 43.8 reduce-scatter.30
  1424.1 46.0 reduce-scatter.34
  1473.8 46.1 reduce-scatter.32
  (6 shorter events, 162.3 us)
